TPU v7x, 128 devices: a whole 4x4x4 slice. The times are simulated.
128 devices in a mesh: group: 8 (over y, core), shard: 16 (over z, x).
Axes of the slice: x: 4, y: 4, z: 4, core: 2. Of those that a mesh axis runs over, the one named last changes fastest.
Arguments:
- query_prefix: bfloat16 [2048, 256], P(('group', 'shard')), may hold values from -6 to 6
- query_tokens: bfloat16 [2048, 32, 128], P(('group', 'shard')), may hold values from -6 to 6
- probes: int32 [2048, 8], P(('group', 'shard')), may hold values from 0 to 63
- candidates: int32 [2048, 8], P(('group', 'shard')), may hold values from 0 to 32767, as said below
- passage_prefix: bfloat16 [32768, 256], P(('group', 'shard')), may hold values from -0.375 to 0.375
- passage_tokens: bfloat16 [32768, 128, 128], P(('group', 'shard')), may hold values from -0.5 to 0.5
Outputs:
- coarse: float32 [2048, 8], P(('group', 'shard'))
- rerank: float32 [2048, 8], P(('group', 'shard'))
Inputs may be any that keep to these rules, and one draw needn't show every extreme that they name: `candidates`: for the 16 queries of one device (rows taken in aligned blocks of 16), at most 2 of their candidate entries lie among the 256 passages of any one device (passages of device d are d * 256 to (d + 1) * 256 - 1, devices numbered group first), and exactly 2 lie on some device.
All inputs are finite; a program needn't handle non-finite values.
Results may differ from a plain program's by a relative error of at most 0.00035.
Values may be sent and summed in bfloat16 or wider, within the bound.
A program may use at most 64 MiB of HBM per device.

v0:
```python
import jax
import jax.numpy as jnp
from jax import lax
from jax.sharding import PartitionSpec as P

CSIZE = 64


def late_scores(token_matrix, passage_texts):
    similarity_values = jnp.einsum(
        "ayo,awo->ayw", token_matrix, passage_texts, preferred_element_type=jnp.float32
    )
    return jnp.mean(jnp.max(similarity_values, axis=-1), axis=-1)


def body(query_prefix, query_tokens, probes, candidates, passage_prefix, passage_tokens):
    shards = lax.axis_size("shard")
    devices = shards * lax.axis_size("group")
    q_rows = query_prefix.shape[0]
    n_cand = candidates.shape[1]
    n_pass = passage_prefix.shape[0]
    n_clusters = n_pass // CSIZE
    tok_len = passage_tokens.shape[1]
    tok_dim = passage_tokens.shape[2]
    group_prefix, group_probes = (
        lax.all_gather(query_prefix, "shard", axis=0, tiled=True),
        lax.all_gather(probes, "shard", axis=0, tiled=True),
    )
    local_ids = lax.axis_index("shard") * n_clusters + jnp.arange(n_clusters, dtype=jnp.int32)
    scores = lax.dot_general(
        group_prefix, passage_prefix, (((1,), (1,)), ((), ())), preferred_element_type=jnp.float32
    )
    best = jnp.max(scores.reshape(q_rows * lax.axis_size("shard"), n_clusters, CSIZE), axis=-1)
    hit = group_probes[:, :, None] == local_ids[None, None, :]
    coarse = lax.psum_scatter(
        jnp.sum(jnp.where(hit, best[:, None, :], jnp.float32(0.0)), axis=-1),
        "shard",
        scatter_dimension=0,
        tiled=True,
    )
    capacity = 2 * q_rows * n_cand // devices
    n_slots = devices * capacity
    flat = candidates.reshape(-1)
    n_req = flat.shape[0]
    source = flat // n_pass
    within = flat % n_pass
    sorted_index_list = jnp.arange(n_req, dtype=jnp.int32)
    earlier = (source[:, None] == source[None, :]) & (
        sorted_index_list[None, :] < sorted_index_list[:, None]
    )
    rank = jnp.sum(earlier.astype(jnp.int32), axis=1)
    slot = source * capacity + rank
    slot_local = jnp.zeros((n_slots,), jnp.int32).at[slot].set(within)
    slot_query = jnp.zeros((n_slots,), jnp.int32).at[slot].set(sorted_index_list // n_cand)
    wanted = lax.all_to_all(
        slot_local.reshape(devices, capacity),
        ("group", "shard"),
        split_axis=0,
        concat_axis=0,
        tiled=True,
    )
    picked = passage_tokens[wanted.reshape(-1)].reshape(devices, capacity, tok_len, tok_dim)
    arrived = lax.all_to_all(picked, ("group", "shard"), split_axis=0, concat_axis=0, tiled=True)
    position_score = late_scores(
        query_tokens[slot_query], arrived.reshape(n_slots, tok_len, tok_dim)
    )
    rerank = position_score[slot].reshape(q_rows, n_cand)
    return (coarse, rerank)


def solution(mesh):
    placed = (
        P(("group", "shard"), None),
        P(("group", "shard"), None, None),
        P(("group", "shard"), None),
        P(("group", "shard"), None),
        P(("group", "shard"), None),
        P(("group", "shard"), None, None),
    )
    return jax.shard_map(
        body,
        mesh=mesh,
        in_specs=placed,
        out_specs=(P(("group", "shard"), None), P(("group", "shard"), None)),
        check_vma=False,
    )
```

profile of v0, /device:TPU:8, one launch (start us, length us, event | category | flops | bytes accessed | tf_op | source)
XLA Modules:
  0.0 242.4 jit_solution(8141240984721965198)
XLA Ops:
  0.6 0.0 copy-start
  0.6 0.8 copy.29
  1.4 0.1 reshape.191
  1.5 0.1 reshape.190
  1.6 0.2 convert_reduce_fusion
  1.8 1.0 scatter_custom_fusion.1
  2.8 0.1 all_to_all.9
  3.0 19.4 %all_to_all.14 = s32[128,1,2]{2,1,0:T(1,128)S(1)} all-to-all(s32[128,1,2]{2,1,0:T(1,128)S(1)} %bitcast.23), channel_id=1, replica_groups=mesh['group'=8,'shard'=16] {'group','shard'}, dimensions={0} | all-to-all | bytes 2048 | tf_op jit(solution)/shard_map/all_to_all | solution.py:55
  22.4 0.5 broadcast.195
  22.9 0.8 reduce.3
  23.7 0.1 reshape.192
  23.9 11.9 %gather_fusion.1 = bf16[256,128,128]{2,1,0:T(8,128)(2,1)} fusion(bf16[256,128,128]{2,1,0:T(8,128)(2,1)} %param.11, s32[1024]{0:T(1024)S(1)} %pad_clamp_fusion.1), kind=kCustom, calls=%fused_computation.1 | custom fusion | bytes 16778240 | tf_op jit(solution)/shard_map/gather | solution.py:62
  35.7 6.3 %all-to-all-start.1 = ((bf16[128,2,128,128]{3,2,1,0:T(8,128)(2,1)}), bf16[128,2,128,128]{3,2,1,0:T(8,128)(2,1)}, u32[]{:S(2)}, u32[]{:S(2)}) async-start(bf16[128,2,128,128]{3,2,1,0:T(8,128)(2,1)} %bitcast.22), calls=%async_computation.1 | async-start | bytes 16777216 | tf_op jit(solution)/shard_map/all_to_all | solution.py:63
  42.0 1.0 scatter_custom_fusion
  43.0 0.0 copy-done.2
  43.0 121.8 %all-gather = s32[16,16,8]{1,2,0:T(8,128)S(1)} all-gather(s32[1,16,8]{1,2,0:T(8,128)S(1)} %bitcast.24), channel_id=1, replica_groups=mesh['group'=8,'shard'=16] {'shard'}, dimensions={0}, use_global_device_ids=true | all-gather | bytes 8704 | tf_op jit(solution)/shard_map/all_gather | solution.py:27
  164.8 0.1 reshape.238
  164.9 0.0 copy-done
  165.0 1.0 gather_fusion
  166.0 0.0 copy-done.4
  166.0 0.6 dynamic-slice
  167.2 25.4 %all_gather.7 = bf16[256,256]{1,0:T(8,128)(2,1)S(1)} all-gather(bf16[16,256]{1,0:T(8,128)(2,1)S(1)} %copy-done.1), channel_id=1, replica_groups=mesh['group'=8,'shard'=16] {'shard'}, dimensions={0}, use_global_device_ids=true | all-gather | bytes 139264 | tf_op jit(solution)/shard_map/all_gather | solution.py:26
  192.6 0.2 bitcast_reduce_fusion
  192.9 0.1 select_reduce_fusion
  192.9 38.6 %all-reduce = f32[256,8]{0,1:T(8,128)S(1)} all-reduce(f32[256,8]{0,1:T(8,128)S(1)} %select_reduce_fusion), channel_id=2, replica_groups=mesh['group'=8,'shard'=16] {'shard'}, use_global_device_ids=true, to_apply=%region_2.3.clone | all-reduce | flops 2048 | bytes 16384
  231.6 0.7 constant_dynamic-slice_fusion
  232.3 0.0 all-to-all-done.1
  232.3 7.9 %convolution_reduce_fusion = f32[256,32]{1,0:T(8,128)S(1)} fusion(bf16[256,32,128]{2,1,0:T(8,128)(2,1)S(1)} %gather_fusion, bf16[256,128,128]{2,1,0:T(8,128)(2,1)} %bitcast.7), kind=kOutput, calls=%fused_computation.5 | convolution fusion | flops 269475840 | bytes 10518528 | tf_op jit(solution)/shard_map/ayo,awo->ayw/dot_general | solution.py:10
  240.2 0.1 reduce_sum.32
  240.3 1.3 gather_fusion.2
  241.6 0.1 reshape.195
  241.7 0.7 copy.33
  (17 shorter events, 0.1 us)
Async XLA Ops:
  0.6 164.3 %copy-start = (bf16[16,32,128]{2,1,0:T(8,128)(2,1)S(1)}, bf16[16,32,128]{2,1,0:T(8,128)(2,1)}, u32[]{:S(2)}) copy-start(bf16[16,32,128]{2,1,0:T(8,128)(2,1)} %param.7) | copy-start | bytes 393220
  35.7 7.3 %copy-start.2 = (s32[16,8]{0,1:T(8,128)S(1)}, s32[16,8]{0,1:T(8,128)}, u32[]{:S(2)}) copy-start(s32[16,8]{0,1:T(8,128)} %param.8) | copy-start | bytes 1540
  35.7 130.3 %copy-start.4 = (u32[128]{0:T(128)S(1)}, u32[128]{0:T(128)}, u32[]{:S(2)}) copy-start(u32[128]{0:T(128)} %constant.69) | copy-start | bytes 1540
  35.7 131.5 %copy-start.1 = (bf16[16,256]{1,0:T(8,128)(2,1)S(1)}, bf16[16,256]{1,0:T(8,128)(2,1)}, u32[]{:S(2)}) copy-start(bf16[16,256]{1,0:T(8,128)(2,1)} %param.6) | copy-start | bytes 24580
  35.7 156.9 %copy-start.3 = (bf16[256,256]{1,0:T(8,128)(2,1)S(1)}, bf16[256,256]{1,0:T(8,128)(2,1)}, u32[]{:S(2)}) copy-start(bf16[256,256]{1,0:T(8,128)(2,1)} %param.10) | copy-start | bytes 393220
  35.7 196.5 %all-to-all-start.1 = ((bf16[128,2,128,128]{3,2,1,0:T(8,128)(2,1)}), bf16[128,2,128,128]{3,2,1,0:T(8,128)(2,1)}, u32[]{:S(2)}, u32[]{:S(2)}) async-start(bf16[128,2,128,128]{3,2,1,0:T(8,128)(2,1)} %bitcast.22), calls=%async_computation.1 | async-start | bytes 16777216 | tf_op jit(solution)/shard_map/all_to_all | solution.py:63
where the time goes:
time: 243 us; the launch traced here: 242 us
  blocking collectives  205 us (84%)
  local copies, waits for them, and re-layouts  20 us (8%)
  matrix products  8.17 us (3%)
  starting transfers between devices  6.26 us (3%)
    all_gather x1, blocking collectives, body(): lax.all_gather(probes, 'shard', axis=0, tiled=True)  122 us
    unnamed x1, blocking collectives  38.6 us
    all_gather x1, blocking collectives, body(): lax.all_gather(query_prefix, 'shard', axis=0, tiled=True)  25.4 us
    all_to_all x1, blocking collectives, body(): lax.all_to_all(slot_local.reshape(devices, capacity), ('group', 'shard'),...  19.4 us
    gather x1, local copies, waits for them, and re-layouts, body(): passage_tokens[wanted.reshape(-1)]  11.9 us
    dot_general x1, matrix products, late_scores(): jnp.einsum('ayo,awo->ayw', token_matrix, passage_texts, preferred_element...  7.93 us
    all_to_all x1, starting transfers between devices, body(): lax.all_to_all(picked, ('group', 'shard'), split_axis=0, concat_axis=0, t...  6.26 us
  transfers between devices with their start and end apart: 1, of which 0 were waited for; matrix products, arithmetic and copies ran while one was open for 2% of the time, Pallas kernels for 0%

commit v1 on v0

v1 whole, which is shorter than its diff:
```python
import functools

import jax
import jax.numpy as jnp
from jax import lax
from jax.experimental import pallas as pl
from jax.experimental.pallas import tpu as pltpu
from jax.sharding import PartitionSpec as P

CSIZE = 64
N_DEV = 128
N_GROUP = 8
N_SHARD = 16
BATCH = 8
N_BATCH = N_DEV // BATCH
MESH = pl.DeviceIdType.MESH


def offsets(j):
    a, b, c, d = j % 4, (j // 4) % 4, (j // 16) % 4, j // 64
    return (a + b + c) % 4, (d + a) % 2, (a + b) % 4, a


def kernel(
    qp_ref, qt_ref, probes_ref, cand_ref, pp_ref, pt_hbm,
    coarse_ref, rerank_ref,
    pt, stage, recv, all_qp, c_stage, c_recv, k_all, sel_v, r_stage, r_recv,
    sel_s, k_smem,
    pt_sem, loc_sem, send_sem, recv_sem, qp_send, qp_recv, ka_send, ka_recv,
    kb_send, kb_recv, c_send, c_rsem, r_send, r_rsem,
):
    g = lax.axis_index("group")
    s = lax.axis_index("shard")
    me = g * N_SHARD + s
    y, core, z, x = g // 2, g % 2, s // 4, s % 4

    def ahead(j):
        dy, dc, dz, dx = offsets(j)
        return ((y + dy) % 4) * 2 + (core + dc) % 2, ((z + dz) % 4) * 4 + (x + dx) % 4

    def behind(j):
        dy, dc, dz, dx = offsets(j)
        return ((y + 4 - dy) % 4) * 2 + (core + dc) % 2, ((z + 4 - dz) % 4) * 4 + (x + 4 - dx) % 4

    pt_copy = pltpu.make_async_copy(pt_hbm, pt, pt_sem)
    pt_copy.start()

    barrier = pltpu.get_barrier_semaphore()

    @pl.loop(1, N_DEV)
    def _(j):
        pl.semaphore_signal(barrier, inc=1, device_id=ahead(j), device_id_type=MESH)

    lane = lax.broadcasted_iota(jnp.int32, (16, 128), 1)
    row = lax.broadcasted_iota(jnp.int32, (16, 128), 0)
    cand = cand_ref[...]
    low = jnp.full((16, 128), 65536.0, jnp.float32)
    high = jnp.full((16, 128), -1.0, jnp.float32)
    for k in range(8):
        c = cand[:, k : k + 1]
        key = ((row * 8 + k) * 256 + (c & 255)).astype(jnp.float32)
        hit = (c >> 8) == lane
        low = jnp.minimum(low, jnp.where(hit, key, 65536.0))
        high = jnp.maximum(high, jnp.where(hit, key, -1.0))
    low = jnp.min(low, axis=0, keepdims=True)
    high = jnp.max(high, axis=0, keepdims=True)
    used = high >= 0.0
    low_i = jnp.where(used, low, 0.0).astype(jnp.int32)
    high_i = jnp.where(used, high, 0.0).astype(jnp.int32)
    sel_v[...] = (low_i >> 11) + (high_i >> 11) * 16
    k_all[me] = (low_i & 255) + (high_i & 255) * 256
    first_flat = low_i >> 8

    sel_copy = pltpu.make_async_copy(sel_v, sel_s, loc_sem)
    sel_copy.start()
    sel_copy.wait()

    v = sel_s[0, me]
    recv[0, 0] = qt_ref[v & 15]
    recv[0, 1] = qt_ref[(v >> 4) & 15]

    @pl.loop(1, N_DEV)
    def _(j):
        dg, ds = ahead(j)
        v = sel_s[0, dg * N_SHARD + ds]
        stage[j, 0] = qt_ref[v & 15]
        stage[j, 1] = qt_ref[(v >> 4) & 15]

    all_qp[s] = qp_ref[...]

    pl.semaphore_wait(barrier, N_DEV - 1)

    @pl.loop(1, N_SHARD)
    def _(i):
        mate = (s + i) % N_SHARD
        pltpu.make_async_remote_copy(
            k_all.at[me], k_all.at[me], ka_send, ka_recv, (g, mate), MESH
        ).start()
        pltpu.make_async_remote_copy(
            qp_ref, all_qp.at[s], qp_send, qp_recv, (g, mate), MESH
        ).start()

    def send_tokens(j):
        pltpu.make_async_remote_copy(
            stage.at[j], recv.at[j], send_sem, recv_sem.at[j // BATCH], ahead(j), MESH
        ).start()

    @pl.loop(1, 32)
    def _(j):
        send_tokens(j)

    pltpu.make_async_copy(k_all.at[pl.ds(0, 15)], k_all.at[pl.ds(0, 15)], ka_recv).wait()

    @pl.loop(1, N_GROUP)
    def _(i):
        rows = k_all.at[pl.ds(g * N_SHARD, N_SHARD)]
        pltpu.make_async_remote_copy(
            rows, rows, kb_send, kb_recv, ((g + i) % N_GROUP, s), MESH
        ).start()

    @pl.loop(32, N_DEV)
    def _(j):
        send_tokens(j)

    pltpu.make_async_copy(all_qp.at[pl.ds(0, 15)], all_qp.at[pl.ds(0, 15)], qp_recv).wait()
    scores = lax.dot_general(
        all_qp[...].reshape(256, 256), pp_ref[...], (((1,), (1,)), ((), ())),
        preferred_element_type=jnp.float32,
    )
    lane2 = lax.broadcasted_iota(jnp.int32, (256, 128), 1)
    best = jnp.zeros((256, 128), jnp.float32)
    for c in range(4):
        half = scores[:, 128 * (c // 2) : 128 * (c // 2) + 128]
        top = jnp.max(jnp.where(lane2 // CSIZE == c % 2, half, -jnp.inf), axis=1, keepdims=True)
        best = jnp.where(lane2 == 4 * s + c, top, best)
    c_stage[...] = best.reshape(16, 16, 128)
    c_recv[s] = c_stage[s]

    @pl.loop(1, N_SHARD)
    def _(i):
        mate = (s + i) % N_SHARD
        pltpu.make_async_remote_copy(
            c_stage.at[mate], c_recv.at[s], c_send, c_rsem, (g, mate), MESH
        ).start()

    pltpu.make_async_copy(k_all.at[pl.ds(0, 112)], k_all.at[pl.ds(0, 112)], kb_recv).wait()
    k_copy = pltpu.make_async_copy(k_all, k_smem, loc_sem)
    k_copy.start()
    k_copy.wait()
    pt_copy.wait()

    lane_r = lax.broadcasted_iota(jnp.int32, (2, 128), 1)

    def score(j):
        bg, bs = behind(j)
        w = k_smem[bg * N_SHARD + bs, 0, me]
        tops = []
        for slot, i in ((0, w & 255), (1, (w >> 8) & 255)):
            sim = lax.dot_general(
                pt[i], recv[j, slot], (((1,), (1,)), ((), ())), preferred_element_type=jnp.float32
            )
            tops.append(jnp.max(sim, axis=0, keepdims=True))
        mean = jnp.sum(jnp.concatenate(tops, axis=0), axis=1, keepdims=True) * (1.0 / 32)
        return jnp.where(lane_r == me, mean, 0.0)

    def back(j):
        pltpu.make_async_remote_copy(
            r_stage.at[j], r_recv.at[j], r_send, r_rsem, behind(j), MESH
        ).start()

    pltpu.make_async_copy(recv.at[pl.ds(1, 7)], recv.at[pl.ds(1, 7)], recv_sem.at[0]).wait()
    r_recv[0] = score(0)
    for j in range(1, BATCH):
        r_stage[j] = score(j)
        back(j)

    @pl.loop(1, N_BATCH)
    def _(b):
        pltpu.make_async_copy(
            recv.at[pl.ds(b * BATCH, BATCH)], recv.at[pl.ds(b * BATCH, BATCH)], recv_sem.at[b]
        ).wait()
        for t in range(BATCH):
            r_stage[b * BATCH + t] = score(b * BATCH + t)
        for t in range(BATCH):
            back(b * BATCH + t)

    lane8 = lax.broadcasted_iota(jnp.int32, (16, 8), 1)

    pltpu.make_async_copy(c_recv.at[pl.ds(0, 15)], c_recv.at[pl.ds(0, 15)], c_rsem).wait()
    all_best = jnp.sum(c_recv[...], axis=0)
    probes = probes_ref[...]
    out = jnp.zeros((16, 8), jnp.float32)
    for k in range(8):
        pick = jnp.sum(jnp.where(probes[:, k : k + 1] == lane, all_best, 0.0), axis=1, keepdims=True)
        out = jnp.where(lane8 == k, pick, out)
    coarse_ref[...] = out

    pltpu.make_async_copy(r_recv.at[pl.ds(1, 127)], r_recv.at[pl.ds(1, 127)], r_rsem).wait()
    both = jnp.sum(r_recv[...], axis=0)
    out = jnp.zeros((16, 8), jnp.float32)
    for k in range(8):
        here = (cand[:, k : k + 1] >> 8) == lane
        value = jnp.where(first_flat == row * 8 + k, both[0:1], both[1:2])
        pick = jnp.sum(jnp.where(here, value, 0.0), axis=1, keepdims=True)
        out = jnp.where(lane8 == k, pick, out)
    rerank_ref[...] = out

    def sent(ref, sem):
        pltpu.make_async_copy(ref, ref, sem).wait()

    sent(stage.at[pl.ds(1, 127)], send_sem)
    sent(all_qp.at[pl.ds(0, 15)], qp_send)
    sent(k_all.at[pl.ds(0, 15)], ka_send)
    sent(k_all.at[pl.ds(0, 112)], kb_send)
    sent(c_recv.at[pl.ds(0, 15)], c_send)
    sent(r_stage.at[pl.ds(1, 127)], r_send)


def body(query_prefix, query_tokens, probes, candidates, passage_prefix, passage_tokens):
    vmem = pl.BlockSpec(memory_space=pltpu.VMEM)
    dma = pltpu.SemaphoreType.DMA
    return tuple(
        pl.pallas_call(
            kernel,
            out_shape=(
                jax.ShapeDtypeStruct((16, 8), jnp.float32),
                jax.ShapeDtypeStruct((16, 8), jnp.float32),
            ),
            in_specs=[vmem] * 5 + [pl.BlockSpec(memory_space=pltpu.HBM)],
            out_specs=(vmem, vmem),
            scratch_shapes=[
                pltpu.VMEM((256, 128, 128), jnp.bfloat16),
                pltpu.VMEM((N_DEV, 2, 32, 128), jnp.bfloat16),
                pltpu.VMEM((N_DEV, 2, 32, 128), jnp.bfloat16),
                pltpu.VMEM((16, 16, 256), jnp.bfloat16),
                pltpu.VMEM((16, 16, 128), jnp.float32),
                pltpu.VMEM((16, 16, 128), jnp.float32),
                pltpu.VMEM((N_DEV, 1, 128), jnp.int32),
                pltpu.VMEM((1, 128), jnp.int32),
                pltpu.VMEM((N_DEV, 2, 128), jnp.float32),
                pltpu.VMEM((N_DEV, 2, 128), jnp.float32),
                pltpu.SMEM((1, 128), jnp.int32),
                pltpu.SMEM((N_DEV, 1, 128), jnp.int32),
                dma, dma, dma, dma((N_BATCH,)), dma, dma, dma, dma, dma, dma, dma, dma, dma, dma,
            ],
            compiler_params=pltpu.CompilerParams(
                collective_id=0, has_side_effects=True, vmem_limit_bytes=48 * 1024 * 1024
            ),
            cost_estimate=pl.CostEstimate(
                flops=300_000_000, bytes_accessed=8_700_000, transcendentals=0
            ),
        )(query_prefix, query_tokens, probes, candidates, passage_prefix, passage_tokens)
    )


def solution(mesh):
    both = ("group", "shard")
    flat, cube = P(both, None), P(both, None, None)
    return jax.shard_map(
        body,
        mesh=mesh,
        in_specs=(flat, cube, flat, flat, flat, cube),
        out_specs=(flat, flat),
        check_vma=False,
    )
```

time: 243 us -> 57.1 us (0.23)
  the two profiles are of different devices: /device:TPU:8 before, /device:TPU:1 now
where the time goes in v1:
time: 57.1 us; the launch traced here: 56.9 us
  Pallas kernels  50.9 us (89%)
  local copies, waits for them, and re-layouts  5.34 us (9%)
  between operations  0.64 us (1%)
    pallas_call x1, Pallas kernels, body(): pl.pallas_call(kernel, out_shape=(jax.ShapeDtypeStruct((16, 8), jnp.float...  50.9 us
    unnamed x8, local copies, waits for them, and re-layouts  4.02 us
    pallas_call x2, local copies, waits for them, and re-layouts, body(): pl.pallas_call(kernel, out_shape=(jax.ShapeDtypeStruct((16, 8), jnp.float...  1.32 us

profile of v1, /device:TPU:1, one launch (start us, length us, event | category | flops | bytes accessed | tf_op | source)
XLA Modules:
  0.0 56.9 jit_solution(8903443776003328991)
XLA Ops:
  0.6 0.8 %copy.8.probes_ref = s32[16,8]{1,0:T(8,128)S(1)} copy(s32[16,8]{0,1:T(8,128)} %param.8) | data formatting | bytes 1024 | tf_op args[2]
  1.4 0.8 %copy.9.cand_ref = s32[16,8]{1,0:T(8,128)S(1)} copy(s32[16,8]{0,1:T(8,128)} %param.9) | data formatting | bytes 1024 | tf_op args[3]
  2.1 0.0 copy-start
  2.1 0.9 %copy-done = bf16[16,32,128]{2,1,0:T(8,128)(2,1)S(1)} copy-done((bf16[16,32,128]{2,1,0:T(8,128)(2,1)S(1)}, bf16[16,32,128]{2,1,0:T(8,128)(2,1)}, u32[]{:S(2)}) %copy-start) | copy-done | bytes 131096
  3.0 0.0 copy-start.1
  3.1 0.9 %copy-done.1 = bf16[256,256]{1,0:T(8,128)(2,1)S(1)} copy-done((bf16[256,256]{1,0:T(8,128)(2,1)S(1)}, bf16[256,256]{1,0:T(8,128)(2,1)}, u32[]{:S(2)}) %copy-start.1) | copy-done | bytes 131096
  4.0 0.0 copy-start.2
  4.0 0.7 %copy-done.2 = bf16[16,256]{1,0:T(8,128)(2,1)S(1)} copy-done((bf16[16,256]{1,0:T(8,128)(2,1)S(1)}, bf16[16,256]{1,0:T(8,128)(2,1)}, u32[]{:S(2)}) %copy-start.2) | copy-done | bytes 8216
  4.7 50.9 %shard_map.77 = (f32[16,8]{1,0:T(8,128)S(1)}, f32[16,8]{1,0:T(8,128)S(1)}) custom-call(bf16[16,256]{1,0:T(8,128)(2,1)S(1)} %copy-done.2, bf16[16,32,128]{2,1,0:T(8,128)(2,1)S(1)} %copy-done, s32[16,8]{1,0:T(8,128)S(1)} %copy.8.probes_ref, s32[16,8]{1,0:T(8,128)S(1)} %copy.9.cand_ref, bf16[256,256]{1,0:T(8,128)(2,1)S(1)} %copy-done.1, ...), custom_call_target="tpu_custom_call" | custom-call | flops 300000000 | bytes 8700000 | tf_op jit(solution)/shard_map/pallas_call | solution.py:223
  55.5 0.7 %copy.10 = f32[16,8]{0,1:T(8,128)} copy(f32[16,8]{1,0:T(8,128)S(1)} %get-tuple-element.2) | data formatting | bytes 1024 | tf_op jit(solution)/shard_map/pallas_call | solution.py:223
  56.2 0.7 %copy.11 = f32[16,8]{0,1:T(8,128)} copy(f32[16,8]{1,0:T(8,128)S(1)} %get-tuple-element.3) | data formatting | bytes 1024 | tf_op jit(solution)/shard_map/pallas_call | solution.py:223
Async XLA Ops:
  2.1 0.9 %copy-start = (bf16[16,32,128]{2,1,0:T(8,128)(2,1)S(1)}, bf16[16,32,128]{2,1,0:T(8,128)(2,1)}, u32[]{:S(2)}) copy-start(bf16[16,32,128]{2,1,0:T(8,128)(2,1)} %qt_ref.1) | copy-start | bytes 393220
  3.0 0.9 %copy-start.1 = (bf16[256,256]{1,0:T(8,128)(2,1)S(1)}, bf16[256,256]{1,0:T(8,128)(2,1)}, u32[]{:S(2)}) copy-start(bf16[256,256]{1,0:T(8,128)(2,1)} %pp_ref.1) | copy-start | bytes 393220
  4.0 0.7 %copy-start.2 = (bf16[16,256]{1,0:T(8,128)(2,1)S(1)}, bf16[16,256]{1,0:T(8,128)(2,1)}, u32[]{:S(2)}) copy-start(bf16[16,256]{1,0:T(8,128)(2,1)} %qp_ref.1) | copy-start | bytes 24580

commit v2 on v1

--- a/solution.py
+++ b/solution.py
@@ -13,20 +13,25 @@
 N_SHARD = 16
 BATCH = 8
 N_BATCH = N_DEV // BATCH
+SPLIT = 64
 MESH = pl.DeviceIdType.MESH
 
 
 def offsets(j):
-    a, b, c, d = j % 4, (j // 4) % 4, (j // 16) % 4, j // 64
-    return (a + b + c) % 4, (d + a) % 2, (a + b) % 4, a
+    a, b, c = (j // 2) % 4, (j // 8) % 4, j // 32
+    return (a + b + c) % 4, j % 2, (a + b) % 4, a
+
+
+def place(dy, dc, dz, dx):
+    return (((dy + 4 - dz) % 4 * 4 + (dz + 4 - dx) % 4) * 4 + dx) * 2 + dc
 
 
 def kernel(
-    qp_ref, qt_ref, probes_ref, cand_ref, pp_ref, pt_hbm,
+    qp_hbm, qt_hbm, probes_hbm, cand_hbm, pp_hbm, pt_hbm,
     coarse_ref, rerank_ref,
-    pt, stage, recv, all_qp, c_stage, c_recv, k_all, sel_v, r_stage, r_recv,
+    qp_ref, qt_ref, probes_ref, cand_ref, pp_ref, pt, stage, recv, all_qp, c_stage, c_recv, k_all, sel_v, r_stage, r_recv,
     sel_s, k_smem,
-    pt_sem, loc_sem, send_sem, recv_sem, qp_send, qp_recv, ka_send, ka_recv,
+    in_sem, loc_sem, ready_sem, send_sem, recv_sem, qp_send, qp_recv, ka_send, ka_recv,
     kb_send, kb_recv, c_send, c_rsem, r_send, r_rsem,
 ):
     g = lax.axis_index("group")
@@ -42,22 +47,48 @@
         dy, dc, dz, dx = offsets(j)
         return ((y + 4 - dy) % 4) * 2 + (core + dc) % 2, ((z + 4 - dz) % 4) * 4 + (x + 4 - dx) % 4
 
-    pt_copy = pltpu.make_async_copy(pt_hbm, pt, pt_sem)
-    pt_copy.start()
-
     barrier = pltpu.get_barrier_semaphore()
 
-    @pl.loop(1, N_DEV)
-    def _(j):
-        pl.semaphore_signal(barrier, inc=1, device_id=ahead(j), device_id_type=MESH)
+    @pl.loop(1, N_SHARD)
+    def _(i):
+        pl.semaphore_signal(
+            barrier, inc=1, device_id=(g, (s + i) % N_SHARD), device_id_type=MESH
+        )
+
+    @pl.loop(1, N_GROUP)
+    def _(i):
+        pl.semaphore_signal(
+            barrier, inc=1, device_id=((g + i) % N_GROUP, s), device_id_type=MESH
+        )
+
+    loads = [
+        pltpu.make_async_copy(src, dst, in_sem.at[i])
+        for i, (src, dst) in enumerate(
+            [(cand_hbm, cand_ref), (qt_hbm, qt_ref), (qp_hbm, qp_ref), (probes_hbm, probes_ref),
+             (pp_hbm, pp_ref), (pt_hbm, pt)]
+        )
+    ]
+    for load in loads:
+        load.start()
+    cand_load, qt_load, qp_load, probes_load, pp_load, pt_load = loads
 
     lane = lax.broadcasted_iota(jnp.int32, (16, 128), 1)
     row = lax.broadcasted_iota(jnp.int32, (16, 128), 0)
-    cand = cand_ref[...]
+    eye = lax.broadcasted_iota(jnp.int32, (16, 16), 0) == lax.broadcasted_iota(jnp.int32, (16, 16), 1)
+
+    def columns(ref):
+        table = ref[...].astype(jnp.float32)
+        return [
+            jnp.sum(jnp.where(eye, table[k : k + 1], 0.0), axis=1, keepdims=True).astype(jnp.int32)
+            for k in range(8)
+        ]
+
+    cand_load.wait()
+    cand = columns(cand_ref)
     low = jnp.full((16, 128), 65536.0, jnp.float32)
     high = jnp.full((16, 128), -1.0, jnp.float32)
     for k in range(8):
-        c = cand[:, k : k + 1]
+        c = cand[k]
         key = ((row * 8 + k) * 256 + (c & 255)).astype(jnp.float32)
         hit = (c >> 8) == lane
         low = jnp.minimum(low, jnp.where(hit, key, 65536.0))
@@ -75,6 +106,7 @@
     sel_copy.start()
     sel_copy.wait()
 
+    qt_load.wait()
     v = sel_s[0, me]
     recv[0, 0] = qt_ref[v & 15]
     recv[0, 1] = qt_ref[(v >> 4) & 15]
@@ -86,18 +118,21 @@
         stage[j, 0] = qt_ref[v & 15]
         stage[j, 1] = qt_ref[(v >> 4) & 15]
 
+    qp_load.wait()
     all_qp[s] = qp_ref[...]
 
-    pl.semaphore_wait(barrier, N_DEV - 1)
-
-    @pl.loop(1, N_SHARD)
-    def _(i):
-        mate = (s + i) % N_SHARD
-        pltpu.make_async_remote_copy(
-            k_all.at[me], k_all.at[me], ka_send, ka_recv, (g, mate), MESH
-        ).start()
-        pltpu.make_async_remote_copy(
-            qp_ref, all_qp.at[s], qp_send, qp_recv, (g, mate), MESH
+    pl.semaphore_wait(barrier, N_SHARD + N_GROUP - 2)
+
+    @pl.loop(1, N_GROUP)
+    def _(i):
+        pl.semaphore_signal(
+            ready_sem, inc=1, device_id=((g + i) % N_GROUP, s), device_id_type=MESH
+        )
+
+    @pl.loop(1, N_SHARD)
+    def _(i):
+        pltpu.make_async_remote_copy(
+            k_all.at[me], k_all.at[me], ka_send, ka_recv, (g, (s + i) % N_SHARD), MESH
         ).start()
 
     def send_tokens(j):
@@ -105,9 +140,20 @@
             stage.at[j], recv.at[j], send_sem, recv_sem.at[j // BATCH], ahead(j), MESH
         ).start()
 
-    @pl.loop(1, 32)
-    def _(j):
-        send_tokens(j)
+    def send_far(j):
+        dy, dc, dz, dx = offsets(j)
+
+        @pl.when(jnp.logical_and(dy + dc > 0, dz + dx > 0))
+        def _():
+            send_tokens(j)
+
+    @pl.loop(1, N_SHARD)
+    def _(i):
+        send_tokens(place(0, 0, i // 4, i % 4))
+
+    @pl.loop(1, N_GROUP)
+    def _(i):
+        send_tokens(place(i // 2, i % 2, 0, 0))
 
     pltpu.make_async_copy(k_all.at[pl.ds(0, 15)], k_all.at[pl.ds(0, 15)], ka_recv).wait()
 
@@ -118,9 +164,22 @@
             rows, rows, kb_send, kb_recv, ((g + i) % N_GROUP, s), MESH
         ).start()
 
-    @pl.loop(32, N_DEV)
-    def _(j):
-        send_tokens(j)
+    @pl.loop(1, N_SHARD)
+    def _(i):
+        pltpu.make_async_remote_copy(
+            qp_ref, all_qp.at[s], qp_send, qp_recv, (g, (s + i) % N_SHARD), MESH
+        ).start()
+
+    pl.semaphore_wait(ready_sem, N_GROUP - 1)
+    pl.loop(1, SPLIT)(send_far)
+
+    pltpu.make_async_copy(k_all.at[pl.ds(0, 112)], k_all.at[pl.ds(0, 112)], kb_recv).wait()
+    k_copy = pltpu.make_async_copy(k_all, k_smem, loc_sem)
+    k_copy.start()
+    k_copy.wait()
+    pl.loop(SPLIT, N_DEV)(send_far)
+
+    pp_load.wait()
 
     pltpu.make_async_copy(all_qp.at[pl.ds(0, 15)], all_qp.at[pl.ds(0, 15)], qp_recv).wait()
     scores = lax.dot_general(
@@ -143,24 +202,30 @@
             c_stage.at[mate], c_recv.at[s], c_send, c_rsem, (g, mate), MESH
         ).start()
 
-    pltpu.make_async_copy(k_all.at[pl.ds(0, 112)], k_all.at[pl.ds(0, 112)], kb_recv).wait()
-    k_copy = pltpu.make_async_copy(k_all, k_smem, loc_sem)
-    k_copy.start()
-    k_copy.wait()
-    pt_copy.wait()
+    pt_load.wait()
 
     lane_r = lax.broadcasted_iota(jnp.int32, (2, 128), 1)
+    own = lax.broadcasted_iota(jnp.int32, (2, 64), 1) // 32 == lax.broadcasted_iota(
+        jnp.int32, (2, 64), 0
+    )
+    none = jnp.zeros((32, 128), jnp.bfloat16)
 
     def score(j):
         bg, bs = behind(j)
         w = k_smem[bg * N_SHARD + bs, 0, me]
-        tops = []
-        for slot, i in ((0, w & 255), (1, (w >> 8) & 255)):
-            sim = lax.dot_general(
-                pt[i], recv[j, slot], (((1,), (1,)), ((), ())), preferred_element_type=jnp.float32
-            )
-            tops.append(jnp.max(sim, axis=0, keepdims=True))
-        mean = jnp.sum(jnp.concatenate(tops, axis=0), axis=1, keepdims=True) * (1.0 / 32)
+        texts = jnp.concatenate([pt[w & 255], pt[(w >> 8) & 255]], axis=1)
+        tokens = jnp.concatenate(
+            [
+                jnp.concatenate([recv[j, 0], none], axis=1),
+                jnp.concatenate([none, recv[j, 1]], axis=1),
+            ],
+            axis=0,
+        )
+        sim = lax.dot_general(
+            texts, tokens, (((1,), (1,)), ((), ())), preferred_element_type=jnp.float32
+        )
+        top = jnp.max(sim, axis=0, keepdims=True)
+        mean = jnp.sum(jnp.where(own, top, 0.0), axis=1, keepdims=True) * (1.0 / 32)
         return jnp.where(lane_r == me, mean, 0.0)
 
     def back(j):
@@ -187,11 +252,12 @@
     lane8 = lax.broadcasted_iota(jnp.int32, (16, 8), 1)
 
     pltpu.make_async_copy(c_recv.at[pl.ds(0, 15)], c_recv.at[pl.ds(0, 15)], c_rsem).wait()
+    probes_load.wait()
     all_best = jnp.sum(c_recv[...], axis=0)
-    probes = probes_ref[...]
+    probes = columns(probes_ref)
     out = jnp.zeros((16, 8), jnp.float32)
     for k in range(8):
-        pick = jnp.sum(jnp.where(probes[:, k : k + 1] == lane, all_best, 0.0), axis=1, keepdims=True)
+        pick = jnp.sum(jnp.where(probes[k] == lane, all_best, 0.0), axis=1, keepdims=True)
         out = jnp.where(lane8 == k, pick, out)
     coarse_ref[...] = out
 
@@ -199,7 +265,7 @@
     both = jnp.sum(r_recv[...], axis=0)
     out = jnp.zeros((16, 8), jnp.float32)
     for k in range(8):
-        here = (cand[:, k : k + 1] >> 8) == lane
+        here = (cand[k] >> 8) == lane
         value = jnp.where(first_flat == row * 8 + k, both[0:1], both[1:2])
         pick = jnp.sum(jnp.where(here, value, 0.0), axis=1, keepdims=True)
         out = jnp.where(lane8 == k, pick, out)
@@ -226,9 +292,14 @@
                 jax.ShapeDtypeStruct((16, 8), jnp.float32),
                 jax.ShapeDtypeStruct((16, 8), jnp.float32),
             ),
-            in_specs=[vmem] * 5 + [pl.BlockSpec(memory_space=pltpu.HBM)],
+            in_specs=[pl.BlockSpec(memory_space=pltpu.HBM)] * 6,
             out_specs=(vmem, vmem),
             scratch_shapes=[
+                pltpu.VMEM((16, 256), jnp.bfloat16),
+                pltpu.VMEM((16, 32, 128), jnp.bfloat16),
+                pltpu.VMEM((8, 16), jnp.int32),
+                pltpu.VMEM((8, 16), jnp.int32),
+                pltpu.VMEM((256, 256), jnp.bfloat16),
                 pltpu.VMEM((256, 128, 128), jnp.bfloat16),
                 pltpu.VMEM((N_DEV, 2, 32, 128), jnp.bfloat16),
                 pltpu.VMEM((N_DEV, 2, 32, 128), jnp.bfloat16),
@@ -241,15 +312,16 @@
                 pltpu.VMEM((N_DEV, 2, 128), jnp.float32),
                 pltpu.SMEM((1, 128), jnp.int32),
                 pltpu.SMEM((N_DEV, 1, 128), jnp.int32),
-                dma, dma, dma, dma((N_BATCH,)), dma, dma, dma, dma, dma, dma, dma, dma, dma, dma,
+                dma((6,)), dma, pltpu.SemaphoreType.REGULAR,
+                dma, dma((N_BATCH,)), dma, dma, dma, dma, dma, dma, dma, dma, dma, dma,
             ],
             compiler_params=pltpu.CompilerParams(
-                collective_id=0, has_side_effects=True, vmem_limit_bytes=48 * 1024 * 1024
+                collective_id=0, has_side_effects=True, vmem_limit_bytes=60 * 1024 * 1024
             ),
             cost_estimate=pl.CostEstimate(
                 flops=300_000_000, bytes_accessed=8_700_000, transcendentals=0
             ),
-        )(query_prefix, query_tokens, probes, candidates, passage_prefix, passage_tokens)
+        )(query_prefix, query_tokens, probes.T, candidates.T, passage_prefix, passage_tokens)
     )
 
 

time: 57.1 us -> 54.1 us (0.947)
  local copies, waits for them, and re-layouts: 5.34 us -> 2.71 us
    unnamed x8 -> x0, local copies, waits for them, and re-layouts: 4.02 us -> none
    pallas_call x2, local copies, waits for them, and re-layouts: 1.32 us -> 2.71 us  [body(): pl.pallas_call(kernel, out_shape=(jax.ShapeDtypeStruct((16, 8), jnp.float...]
where the time goes in v2:
time: 54.1 us; the launch traced here: 53.8 us
  Pallas kernels  50.5 us (93%)
  local copies, waits for them, and re-layouts  2.71 us (5%)
  between operations  0.64 us (1%)
    pallas_call x1, Pallas kernels, body(): pl.pallas_call(kernel, out_shape=(jax.ShapeDtypeStruct((16, 8), jnp.float...  50.5 us
    pallas_call x2, local copies, waits for them, and re-layouts, body(): pl.pallas_call(kernel, out_shape=(jax.ShapeDtypeStruct((16, 8), jnp.float...  2.71 us

profile of v2, /device:TPU:1, one launch (start us, length us, event | category | flops | bytes accessed | tf_op | source)
XLA Modules:
  0.0 53.8 jit_solution(16508659109436025459)
XLA Ops:
  0.6 50.5 %shard_map.77 = (f32[16,8]{1,0:T(8,128)}, f32[16,8]{1,0:T(8,128)}) custom-call(bf16[16,256]{1,0:T(8,128)(2,1)} %qp_hbm.1, bf16[16,32,128]{2,1,0:T(8,128)(2,1)} %qt_hbm.1, s32[8,16]{1,0:T(8,128)} %bitcast.2, s32[8,16]{1,0:T(8,128)} %bitcast.3, bf16[256,256]{1,0:T(8,128)(2,1)} %pp_hbm.1, bf16[256,128,128]{2,1,0:T(8,128)(2,1)} %pt_hbm.1), custom_call_target="tpu_custom_call" | custom-call | flops 300000000 | bytes 8700000 | tf_op jit(solution)/shard_map/pallas_call | solution.py:289
  51.1 1.4 %copy.8 = f32[16,8]{0,1:T(8,128)} copy(f32[16,8]{1,0:T(8,128)} %get-tuple-element.2) | data formatting | bytes 1024 | tf_op jit(solution)/shard_map/pallas_call | solution.py:289
  52.5 1.4 %copy.9 = f32[16,8]{0,1:T(8,128)} copy(f32[16,8]{1,0:T(8,128)} %get-tuple-element.3) | data formatting | bytes 1024 | tf_op jit(solution)/shard_map/pallas_call | solution.py:289

commit v3 on v2

--- a/solution.py
+++ b/solution.py
@@ -11,28 +11,33 @@
 N_DEV = 128
 N_GROUP = 8
 N_SHARD = 16
-BATCH = 8
+BATCH = 16
+HALF = BATCH // 2
+LEAD = 16
 N_BATCH = N_DEV // BATCH
-SPLIT = 64
 MESH = pl.DeviceIdType.MESH
 
 
+def mod4(n):
+    return lax.rem(n, 4)
+
+
 def offsets(j):
-    a, b, c = (j // 2) % 4, (j // 8) % 4, j // 32
-    return (a + b + c) % 4, j % 2, (a + b) % 4, a
+    a, b, c = mod4(lax.div(j, 2)), mod4(lax.div(j, 8)), lax.div(j, 32)
+    return mod4(a + b + c), lax.rem(j, 2), mod4(a + b), a
 
 
 def place(dy, dc, dz, dx):
-    return (((dy + 4 - dz) % 4 * 4 + (dz + 4 - dx) % 4) * 4 + dx) * 2 + dc
+    return ((mod4(dy + 4 - dz) * 4 + mod4(dz + 4 - dx)) * 4 + dx) * 2 + dc
 
 
 def kernel(
     qp_hbm, qt_hbm, probes_hbm, cand_hbm, pp_hbm, pt_hbm,
     coarse_ref, rerank_ref,
-    qp_ref, qt_ref, probes_ref, cand_ref, pp_ref, pt, stage, recv, all_qp, c_stage, c_recv, k_all, sel_v, r_stage, r_recv,
+    qp_ref, qt_ref, probes_ref, cand_ref, pp_ref, pt, stage, recv, all_qp, c_stage, c_recv, sel_v, key_v, k_all, r_stage, r_recv,
     sel_s, k_smem,
-    in_sem, loc_sem, ready_sem, send_sem, recv_sem, qp_send, qp_recv, ka_send, ka_recv,
-    kb_send, kb_recv, c_send, c_rsem, r_send, r_rsem,
+    in_sem, loc_sem, k_sem, ready_sem, send_sem, recv_sem, qp_send, qp_recv, k_send, k_recv,
+    c_send, c_rsem, r_send, r_rsem,
 ):
     g = lax.axis_index("group")
     s = lax.axis_index("shard")
@@ -41,11 +46,11 @@
 
     def ahead(j):
         dy, dc, dz, dx = offsets(j)
-        return ((y + dy) % 4) * 2 + (core + dc) % 2, ((z + dz) % 4) * 4 + (x + dx) % 4
+        return mod4(y + dy) * 2 + lax.rem(core + dc, 2), mod4(z + dz) * 4 + mod4(x + dx)
 
     def behind(j):
         dy, dc, dz, dx = offsets(j)
-        return ((y + 4 - dy) % 4) * 2 + (core + dc) % 2, ((z + 4 - dz) % 4) * 4 + (x + 4 - dx) % 4
+        return mod4(y + 4 - dy) * 2 + lax.rem(core + dc, 2), mod4(z + 4 - dz) * 4 + mod4(x + 4 - dx)
 
     barrier = pltpu.get_barrier_semaphore()
 
@@ -99,7 +104,9 @@
     low_i = jnp.where(used, low, 0.0).astype(jnp.int32)
     high_i = jnp.where(used, high, 0.0).astype(jnp.int32)
     sel_v[...] = (low_i >> 11) + (high_i >> 11) * 16
-    k_all[me] = (low_i & 255) + (high_i & 255) * 256
+    key = (low_i & 255) + (high_i & 255) * 256
+    key_v[...] = key
+    k_all[0] = key
     first_flat = low_i >> 8
 
     sel_copy = pltpu.make_async_copy(sel_v, sel_s, loc_sem)
@@ -129,55 +136,60 @@
             ready_sem, inc=1, device_id=((g + i) % N_GROUP, s), device_id_type=MESH
         )
 
+    def send_key(j):
+        pltpu.make_async_remote_copy(
+            key_v, k_all.at[j], k_send, k_recv.at[lax.div(j, BATCH)], ahead(j), MESH
+        ).start()
+
+    def send_tokens(j):
+        pltpu.make_async_remote_copy(
+            stage.at[j], recv.at[j], send_sem, recv_sem.at[lax.div(j, HALF)], ahead(j), MESH
+        ).start()
+
+    def mates(send):
+        @pl.loop(1, N_SHARD)
+        def _(i):
+            send(place(0, 0, lax.div(i, 4), mod4(i)))
+
+        @pl.loop(1, N_GROUP)
+        def _(i):
+            send(place(lax.div(i, 2), lax.rem(i, 2), 0, 0))
+
+    def other(send):
+        def guarded(j):
+            dy, dc, dz, dx = offsets(j)
+
+            @pl.when(jnp.logical_and(dy + dc > 0, dz + dx > 0))
+            def _():
+                send(j)
+
+        return guarded
+
+    mates(send_key)
+
     @pl.loop(1, N_SHARD)
     def _(i):
         pltpu.make_async_remote_copy(
-            k_all.at[me], k_all.at[me], ka_send, ka_recv, (g, (s + i) % N_SHARD), MESH
-        ).start()
-
-    def send_tokens(j):
-        pltpu.make_async_remote_copy(
-            stage.at[j], recv.at[j], send_sem, recv_sem.at[j // BATCH], ahead(j), MESH
-        ).start()
-
-    def send_far(j):
-        dy, dc, dz, dx = offsets(j)
-
-        @pl.when(jnp.logical_and(dy + dc > 0, dz + dx > 0))
-        def _():
-            send_tokens(j)
-
-    @pl.loop(1, N_SHARD)
-    def _(i):
-        send_tokens(place(0, 0, i // 4, i % 4))
-
-    @pl.loop(1, N_GROUP)
-    def _(i):
-        send_tokens(place(i // 2, i % 2, 0, 0))
-
-    pltpu.make_async_copy(k_all.at[pl.ds(0, 15)], k_all.at[pl.ds(0, 15)], ka_recv).wait()
-
-    @pl.loop(1, N_GROUP)
-    def _(i):
-        rows = k_all.at[pl.ds(g * N_SHARD, N_SHARD)]
-        pltpu.make_async_remote_copy(
-            rows, rows, kb_send, kb_recv, ((g + i) % N_GROUP, s), MESH
-        ).start()
-
-    @pl.loop(1, N_SHARD)
-    def _(i):
-        pltpu.make_async_remote_copy(
-            qp_ref, all_qp.at[s], qp_send, qp_recv, (g, (s + i) % N_SHARD), MESH
-        ).start()
-
+            qp_ref, all_qp.at[s], qp_send, qp_recv, (g, lax.rem(s + i, N_SHARD)), MESH
+        ).start()
+
+    mates(send_tokens)
     pl.semaphore_wait(ready_sem, N_GROUP - 1)
-    pl.loop(1, SPLIT)(send_far)
-
-    pltpu.make_async_copy(k_all.at[pl.ds(0, 112)], k_all.at[pl.ds(0, 112)], kb_recv).wait()
-    k_copy = pltpu.make_async_copy(k_all, k_smem, loc_sem)
-    k_copy.start()
-    k_copy.wait()
-    pl.loop(SPLIT, N_DEV)(send_far)
+    pl.loop(1, LEAD)(other(send_key))
+
+    @pl.loop(LEAD, N_DEV)
+    def _(j):
+        other(send_key)(j)
+        other(send_tokens)(j - LEAD)
+
+    pl.loop(N_DEV - LEAD, N_DEV)(other(send_tokens))
+
+    def key_rows(b):
+        rows = pl.ds(b * BATCH, BATCH)
+        return pltpu.make_async_copy(k_all.at[rows], k_smem.at[rows], k_sem.at[b])
+
+    pltpu.make_async_copy(k_all.at[pl.ds(1, BATCH - 1)], k_all.at[pl.ds(1, BATCH - 1)], k_recv.at[0]).wait()
+    key_rows(0).start()
 
     pp_load.wait()
 
@@ -211,8 +223,7 @@
     none = jnp.zeros((32, 128), jnp.bfloat16)
 
     def score(j):
-        bg, bs = behind(j)
-        w = k_smem[bg * N_SHARD + bs, 0, me]
+        w = k_smem[j, 0, me]
         texts = jnp.concatenate([pt[w & 255], pt[(w >> 8) & 255]], axis=1)
         tokens = jnp.concatenate(
             [
@@ -233,21 +244,47 @@
             r_stage.at[j], r_recv.at[j], r_send, r_rsem, behind(j), MESH
         ).start()
 
-    pltpu.make_async_copy(recv.at[pl.ds(1, 7)], recv.at[pl.ds(1, 7)], recv_sem.at[0]).wait()
-    r_recv[0] = score(0)
-    for j in range(1, BATCH):
-        r_stage[j] = score(j)
-        back(j)
-
-    @pl.loop(1, N_BATCH)
+    def arrived(first, count, h):
+        rows = recv.at[pl.ds(first, count)]
+        pltpu.make_async_copy(rows, rows, recv_sem.at[h]).wait()
+
+    def batch(first, count):
+        for t in range(count):
+            r_stage[first + t] = score(first + t)
+
+    def next_keys(b):
+        rows = k_all.at[pl.ds(b * BATCH, BATCH)]
+        pltpu.make_async_copy(rows, rows, k_recv.at[b]).wait()
+        key_rows(b).start()
+
+    key_rows(0).wait()
+    arrived(1, HALF - 1, 0)
+    next_keys(1)
+    batch(0, HALF)
+    arrived(HALF, HALF, 1)
+    batch(HALF, HALF)
+    r_recv[0] = r_stage[0]
+    pl.loop(1, BATCH)(back)
+
+    @pl.loop(1, N_BATCH - 1)
     def _(b):
-        pltpu.make_async_copy(
-            recv.at[pl.ds(b * BATCH, BATCH)], recv.at[pl.ds(b * BATCH, BATCH)], recv_sem.at[b]
-        ).wait()
+        first = b * BATCH
+        arrived(first, HALF, 2 * b)
+        arrived(first + HALF, HALF, 2 * b + 1)
+        next_keys(b + 1)
+        key_rows(b).wait()
+        batch(first, BATCH)
         for t in range(BATCH):
-            r_stage[b * BATCH + t] = score(b * BATCH + t)
-        for t in range(BATCH):
-            back(b * BATCH + t)
+            back(first + t)
+
+    key_rows(N_BATCH - 1).wait()
+
+    @pl.loop(2 * N_BATCH - 2, 2 * N_BATCH)
+    def _(h):
+        arrived(h * HALF, HALF, h)
+        batch(h * HALF, HALF)
+        for t in range(HALF):
+            back(h * HALF + t)
 
     lane8 = lax.broadcasted_iota(jnp.int32, (16, 8), 1)
 
@@ -276,8 +313,7 @@
 
     sent(stage.at[pl.ds(1, 127)], send_sem)
     sent(all_qp.at[pl.ds(0, 15)], qp_send)
-    sent(k_all.at[pl.ds(0, 15)], ka_send)
-    sent(k_all.at[pl.ds(0, 112)], kb_send)
+    sent(k_all.at[pl.ds(1, 127)], k_send)
     sent(c_recv.at[pl.ds(0, 15)], c_send)
     sent(r_stage.at[pl.ds(1, 127)], r_send)
 
@@ -306,14 +342,15 @@
                 pltpu.VMEM((16, 16, 256), jnp.bfloat16),
                 pltpu.VMEM((16, 16, 128), jnp.float32),
                 pltpu.VMEM((16, 16, 128), jnp.float32),
+                pltpu.VMEM((1, 128), jnp.int32),
+                pltpu.VMEM((1, 128), jnp.int32),
                 pltpu.VMEM((N_DEV, 1, 128), jnp.int32),
-                pltpu.VMEM((1, 128), jnp.int32),
                 pltpu.VMEM((N_DEV, 2, 128), jnp.float32),
                 pltpu.VMEM((N_DEV, 2, 128), jnp.float32),
                 pltpu.SMEM((1, 128), jnp.int32),
                 pltpu.SMEM((N_DEV, 1, 128), jnp.int32),
-                dma((6,)), dma, pltpu.SemaphoreType.REGULAR,
-                dma, dma((N_BATCH,)), dma, dma, dma, dma, dma, dma, dma, dma, dma, dma,
+                dma((6,)), dma, dma((N_BATCH,)), pltpu.SemaphoreType.REGULAR,
+                dma, dma((2 * N_BATCH,)), dma, dma, dma, dma((N_BATCH,)), dma, dma, dma, dma,
             ],
             compiler_params=pltpu.CompilerParams(
                 collective_id=0, has_side_effects=True, vmem_limit_bytes=60 * 1024 * 1024

time: 54.1 us -> 53.1 us (0.982)
  Pallas kernels: 50.5 us -> 49.5 us
    pallas_call x1, Pallas kernels: 50.5 us -> 49.5 us  [body(): pl.pallas_call(kernel, out_shape=(jax.ShapeDtypeStruct((16, 8), jnp.float...]
where the time goes in v3:
time: 53.1 us; the launch traced here: 52.9 us
  Pallas kernels  49.5 us (93%)
  local copies, waits for them, and re-layouts  2.71 us (5%)
  between operations  0.64 us (1%)
    pallas_call x1, Pallas kernels, body(): pl.pallas_call(kernel, out_shape=(jax.ShapeDtypeStruct((16, 8), jnp.float...  49.5 us
    pallas_call x2, local copies, waits for them, and re-layouts, body(): pl.pallas_call(kernel, out_shape=(jax.ShapeDtypeStruct((16, 8), jnp.float...  2.71 us

profile of v3, /device:TPU:1, one launch (start us, length us, event | category | flops | bytes accessed | tf_op | source)
XLA Modules:
  0.0 52.9 jit_solution(11301786178342019266)
XLA Ops:
  0.6 49.5 %shard_map.77 = (f32[16,8]{1,0:T(8,128)}, f32[16,8]{1,0:T(8,128)}) custom-call(bf16[16,256]{1,0:T(8,128)(2,1)} %qp_hbm.1, bf16[16,32,128]{2,1,0:T(8,128)(2,1)} %qt_hbm.1, s32[8,16]{1,0:T(8,128)} %bitcast.2, s32[8,16]{1,0:T(8,128)} %bitcast.3, bf16[256,256]{1,0:T(8,128)(2,1)} %pp_hbm.1, bf16[256,128,128]{2,1,0:T(8,128)(2,1)} %pt_hbm.1), custom_call_target="tpu_custom_call" | custom-call | flops 300000000 | bytes 8700000 | tf_op jit(solution)/shard_map/pallas_call | solution.py:325
  50.2 1.4 %copy.8 = f32[16,8]{0,1:T(8,128)} copy(f32[16,8]{1,0:T(8,128)} %get-tuple-element.2) | data formatting | bytes 1024 | tf_op jit(solution)/shard_map/pallas_call | solution.py:325
  51.5 1.4 %copy.9 = f32[16,8]{0,1:T(8,128)} copy(f32[16,8]{1,0:T(8,128)} %get-tuple-element.3) | data formatting | bytes 1024 | tf_op jit(solution)/shard_map/pallas_call | solution.py:325

commit v4 on v3

--- a/solution.py
+++ b/solution.py
@@ -18,22 +18,25 @@
 MESH = pl.DeviceIdType.MESH
 
 
-def mod4(n):
-    return lax.rem(n, 4)
-
-
-def offsets(j):
-    a, b, c = mod4(lax.div(j, 2)), mod4(lax.div(j, 8)), lax.div(j, 32)
-    return mod4(a + b + c), lax.rem(j, 2), mod4(a + b), a
-
-
-def place(dy, dc, dz, dx):
-    return ((mod4(dy + 4 - dz) * 4 + mod4(dz + 4 - dx)) * 4 + dx) * 2 + dc
+def relative_places():
+    steps = [
+        (dy, dc, dz, dx) for dy in range(4) for dc in range(2) for dz in range(4) for dx in range(4)
+    ]
+    near = [0, 1, 2, 1]
+    shuffled = [steps[37 * i % N_DEV] for i in range(N_DEV)]
+    shuffled.sort(key=lambda o: -(near[o[0]] + near[o[2]] + near[o[3]]))
+    is_mate = lambda o: o[0] + o[1] == 0 or o[2] + o[3] == 0
+    mates = [o for o in shuffled if is_mate(o) and any(o)]
+    return [(0, 0, 0, 0)] + mates + [o for o in shuffled if not is_mate(o)]
+
+
+PLACES = relative_places()
+N_MATES = N_GROUP + N_SHARD - 1
 
 
 def kernel(
     qp_hbm, qt_hbm, probes_hbm, cand_hbm, pp_hbm, pt_hbm,
-    coarse_ref, rerank_ref,
+    out_ref,
     qp_ref, qt_ref, probes_ref, cand_ref, pp_ref, pt, stage, recv, all_qp, c_stage, c_recv, sel_v, key_v, k_all, r_stage, r_recv,
     sel_s, k_smem,
     in_sem, loc_sem, k_sem, ready_sem, send_sem, recv_sem, qp_send, qp_recv, k_send, k_recv,
@@ -44,13 +47,18 @@
     me = g * N_SHARD + s
     y, core, z, x = g // 2, g % 2, s // 4, s % 4
 
+    ys = [lax.rem(y + k, 4) * 2 for k in range(4)]
+    cores = [core, 1 - core]
+    zs = [lax.rem(z + k, 4) * 4 for k in range(4)]
+    xs = [lax.rem(x + k, 4) for k in range(4)]
+
     def ahead(j):
-        dy, dc, dz, dx = offsets(j)
-        return mod4(y + dy) * 2 + lax.rem(core + dc, 2), mod4(z + dz) * 4 + mod4(x + dx)
+        dy, dc, dz, dx = PLACES[j]
+        return ys[dy] + cores[dc], zs[dz] + xs[dx]
 
     def behind(j):
-        dy, dc, dz, dx = offsets(j)
-        return mod4(y + 4 - dy) * 2 + lax.rem(core + dc, 2), mod4(z + 4 - dz) * 4 + mod4(x + 4 - dx)
+        dy, dc, dz, dx = PLACES[j]
+        return ys[-dy % 4] + cores[dc], zs[-dz % 4] + xs[-dx % 4]
 
     barrier = pltpu.get_barrier_semaphore()
 
@@ -118,13 +126,15 @@
     recv[0, 0] = qt_ref[v & 15]
     recv[0, 1] = qt_ref[(v >> 4) & 15]
 
-    @pl.loop(1, N_DEV)
-    def _(j):
+    def fill(j):
         dg, ds = ahead(j)
         v = sel_s[0, dg * N_SHARD + ds]
         stage[j, 0] = qt_ref[v & 15]
         stage[j, 1] = qt_ref[(v >> 4) & 15]
 
+    for j in range(1, N_MATES):
+        fill(j)
+
     qp_load.wait()
     all_qp[s] = qp_ref[...]
 
@@ -138,34 +148,16 @@
 
     def send_key(j):
         pltpu.make_async_remote_copy(
-            key_v, k_all.at[j], k_send, k_recv.at[lax.div(j, BATCH)], ahead(j), MESH
+            key_v, k_all.at[j], k_send, k_recv.at[j // BATCH], ahead(j), MESH
         ).start()
 
     def send_tokens(j):
         pltpu.make_async_remote_copy(
-            stage.at[j], recv.at[j], send_sem, recv_sem.at[lax.div(j, HALF)], ahead(j), MESH
-        ).start()
-
-    def mates(send):
-        @pl.loop(1, N_SHARD)
-        def _(i):
-            send(place(0, 0, lax.div(i, 4), mod4(i)))
-
-        @pl.loop(1, N_GROUP)
-        def _(i):
-            send(place(lax.div(i, 2), lax.rem(i, 2), 0, 0))
-
-    def other(send):
-        def guarded(j):
-            dy, dc, dz, dx = offsets(j)
-
-            @pl.when(jnp.logical_and(dy + dc > 0, dz + dx > 0))
-            def _():
-                send(j)
-
-        return guarded
-
-    mates(send_key)
+            stage.at[j], recv.at[j], send_sem, recv_sem.at[j // HALF], ahead(j), MESH
+        ).start()
+
+    for j in range(1, N_MATES):
+        send_key(j)
 
     @pl.loop(1, N_SHARD)
     def _(i):
@@ -173,16 +165,16 @@
             qp_ref, all_qp.at[s], qp_send, qp_recv, (g, lax.rem(s + i, N_SHARD)), MESH
         ).start()
 
-    mates(send_tokens)
+    for j in range(1, N_MATES):
+        send_tokens(j)
+    for j in range(N_MATES, N_DEV):
+        fill(j)
     pl.semaphore_wait(ready_sem, N_GROUP - 1)
-    pl.loop(1, LEAD)(other(send_key))
-
-    @pl.loop(LEAD, N_DEV)
-    def _(j):
-        other(send_key)(j)
-        other(send_tokens)(j - LEAD)
-
-    pl.loop(N_DEV - LEAD, N_DEV)(other(send_tokens))
+    for j in range(N_MATES, N_DEV + LEAD):
+        if j < N_DEV:
+            send_key(j)
+        if j >= N_MATES + LEAD:
+            send_tokens(j - LEAD)
 
     def key_rows(b):
         rows = pl.ds(b * BATCH, BATCH)
@@ -264,7 +256,8 @@
     arrived(HALF, HALF, 1)
     batch(HALF, HALF)
     r_recv[0] = r_stage[0]
-    pl.loop(1, BATCH)(back)
+    for j in range(1, BATCH):
+        back(j)
 
     @pl.loop(1, N_BATCH - 1)
     def _(b):
@@ -274,8 +267,12 @@
         next_keys(b + 1)
         key_rows(b).wait()
         batch(first, BATCH)
-        for t in range(BATCH):
-            back(first + t)
+        for n in range(1, N_BATCH - 1):
+
+            @pl.when(b == n)
+            def _():
+                for j in range(n * BATCH, (n + 1) * BATCH):
+                    back(j)
 
     key_rows(N_BATCH - 1).wait()
 
@@ -283,30 +280,38 @@
     def _(h):
         arrived(h * HALF, HALF, h)
         batch(h * HALF, HALF)
-        for t in range(HALF):
-            back(h * HALF + t)
-
-    lane8 = lax.broadcasted_iota(jnp.int32, (16, 8), 1)
+        for n in (2 * N_BATCH - 2, 2 * N_BATCH - 1):
+
+            @pl.when(h == n)
+            def _():
+                for j in range(n * HALF, (n + 1) * HALF):
+                    back(j)
+
+    row8 = lax.broadcasted_iota(jnp.int32, (8, 16), 0)
+
+    def across(column):
+        return jnp.sum(jnp.where(eye, column, 0.0), axis=0, keepdims=True)
+
 
     pltpu.make_async_copy(c_recv.at[pl.ds(0, 15)], c_recv.at[pl.ds(0, 15)], c_rsem).wait()
     probes_load.wait()
     all_best = jnp.sum(c_recv[...], axis=0)
     probes = columns(probes_ref)
-    out = jnp.zeros((16, 8), jnp.float32)
+    out = jnp.zeros((8, 16), jnp.float32)
     for k in range(8):
         pick = jnp.sum(jnp.where(probes[k] == lane, all_best, 0.0), axis=1, keepdims=True)
-        out = jnp.where(lane8 == k, pick, out)
-    coarse_ref[...] = out
+        out = jnp.where(row8 == k, across(pick), out)
+    out_ref[0] = out
 
     pltpu.make_async_copy(r_recv.at[pl.ds(1, 127)], r_recv.at[pl.ds(1, 127)], r_rsem).wait()
     both = jnp.sum(r_recv[...], axis=0)
-    out = jnp.zeros((16, 8), jnp.float32)
+    out = jnp.zeros((8, 16), jnp.float32)
     for k in range(8):
         here = (cand[k] >> 8) == lane
         value = jnp.where(first_flat == row * 8 + k, both[0:1], both[1:2])
         pick = jnp.sum(jnp.where(here, value, 0.0), axis=1, keepdims=True)
-        out = jnp.where(lane8 == k, pick, out)
-    rerank_ref[...] = out
+        out = jnp.where(row8 == k, across(pick), out)
+    out_ref[1] = out
 
     def sent(ref, sem):
         pltpu.make_async_copy(ref, ref, sem).wait()
@@ -321,15 +326,12 @@
 def body(query_prefix, query_tokens, probes, candidates, passage_prefix, passage_tokens):
     vmem = pl.BlockSpec(memory_space=pltpu.VMEM)
     dma = pltpu.SemaphoreType.DMA
-    return tuple(
+    scores = (
         pl.pallas_call(
             kernel,
-            out_shape=(
-                jax.ShapeDtypeStruct((16, 8), jnp.float32),
-                jax.ShapeDtypeStruct((16, 8), jnp.float32),
-            ),
+            out_shape=jax.ShapeDtypeStruct((2, 8, 16), jnp.float32),
             in_specs=[pl.BlockSpec(memory_space=pltpu.HBM)] * 6,
-            out_specs=(vmem, vmem),
+            out_specs=vmem,
             scratch_shapes=[
                 pltpu.VMEM((16, 256), jnp.bfloat16),
                 pltpu.VMEM((16, 32, 128), jnp.bfloat16),
@@ -360,6 +362,7 @@
             ),
         )(query_prefix, query_tokens, probes.T, candidates.T, passage_prefix, passage_tokens)
     )
+    return scores[0].T, scores[1].T
 
 
 def solution(mesh):

time: 53.1 us -> 46.3 us (0.87)
  Pallas kernels: 49.5 us -> 44.2 us
  local copies, waits for them, and re-layouts: 2.71 us -> 1.28 us
    pallas_call x1, Pallas kernels: 49.5 us -> 44.2 us  [body(): pl.pallas_call(kernel, out_shape=jax.ShapeDtypeStruct((2, 8, 16), jnp.flo...]
    pallas_call x2 -> x0, local copies, waits for them, and re-layouts: 2.71 us -> none  [body(): pl.pallas_call(kernel, out_shape=(jax.ShapeDtypeStruct((16, 8), jnp.float...]
    transpose x0 -> x1, local copies, waits for them, and re-layouts: none -> 1.28 us  [body(): return (scores[0].T, scores[1].T)]
where the time goes in v4:
time: 46.3 us; the launch traced here: 46.1 us
  Pallas kernels  44.2 us (95%)
  local copies, waits for them, and re-layouts  1.28 us (3%)
  between operations  0.64 us (1%)
    pallas_call x1, Pallas kernels, body(): pl.pallas_call(kernel, out_shape=jax.ShapeDtypeStruct((2, 8, 16), jnp.flo...  44.2 us
    transpose x1, local copies, waits for them, and re-layouts, body(): return (scores[0].T, scores[1].T)  1.28 us

profile of v4, /device:TPU:1, one launch (start us, length us, event | category | flops | bytes accessed | tf_op | source)
XLA Modules:
  0.0 46.1 jit_solution(7645507454818801844)
XLA Ops:
  0.6 44.2 %shard_map.77 = f32[2,8,16]{2,1,0:T(8,128)} custom-call(bf16[16,256]{1,0:T(8,128)(2,1)} %qp_hbm.1, bf16[16,32,128]{2,1,0:T(8,128)(2,1)} %qt_hbm.1, s32[8,16]{1,0:T(8,128)} %bitcast.10, s32[8,16]{1,0:T(8,128)} %bitcast.11, bf16[256,256]{1,0:T(8,128)(2,1)} %pp_hbm.1, bf16[256,128,128]{2,1,0:T(8,128)(2,1)} %pt_hbm.1), custom_call_target="tpu_custom_call" | custom-call | flops 300000000 | bytes 8700000 | tf_op jit(solution)/shard_map/pallas_call | solution.py:330
  44.8 1.3 %slice_bitcast_fusion = (f32[16,8]{0,1:T(8,128)}, f32[16,8]{0,1:T(8,128)}) fusion(f32[2,8,16]{2,1,0:T(8,128)} %shard_map.77), kind=kLoop, calls=%fused_computation | loop fusion | bytes 2048 | tf_op jit(solution)/shard_map/transpose | solution.py:365

commit v5 on v4

--- a/solution.py
+++ b/solution.py
@@ -31,6 +31,8 @@
 
 
 PLACES = relative_places()
+SHARD_MATES = [j for j, o in enumerate(PLACES) if any(o) and o[0] + o[1] == 0]
+GROUP_MATES = [j for j, o in enumerate(PLACES) if any(o) and o[2] + o[3] == 0]
 N_MATES = N_GROUP + N_SHARD - 1
 
 
@@ -60,20 +62,6 @@
         dy, dc, dz, dx = PLACES[j]
         return ys[-dy % 4] + cores[dc], zs[-dz % 4] + xs[-dx % 4]
 
-    barrier = pltpu.get_barrier_semaphore()
-
-    @pl.loop(1, N_SHARD)
-    def _(i):
-        pl.semaphore_signal(
-            barrier, inc=1, device_id=(g, (s + i) % N_SHARD), device_id_type=MESH
-        )
-
-    @pl.loop(1, N_GROUP)
-    def _(i):
-        pl.semaphore_signal(
-            barrier, inc=1, device_id=((g + i) % N_GROUP, s), device_id_type=MESH
-        )
-
     loads = [
         pltpu.make_async_copy(src, dst, in_sem.at[i])
         for i, (src, dst) in enumerate(
@@ -81,7 +69,13 @@
              (pp_hbm, pp_ref), (pt_hbm, pt)]
         )
     ]
-    for load in loads:
+    for load in loads[:2]:
+        load.start()
+
+    barrier = pltpu.get_barrier_semaphore()
+    for j in range(1, N_MATES):
+        pl.semaphore_signal(barrier, inc=1, device_id=ahead(j), device_id_type=MESH)
+    for load in loads[2:]:
         load.start()
     cand_load, qt_load, qp_load, probes_load, pp_load, pt_load = loads
 
@@ -138,13 +132,9 @@
     qp_load.wait()
     all_qp[s] = qp_ref[...]
 
-    pl.semaphore_wait(barrier, N_SHARD + N_GROUP - 2)
-
-    @pl.loop(1, N_GROUP)
-    def _(i):
-        pl.semaphore_signal(
-            ready_sem, inc=1, device_id=((g + i) % N_GROUP, s), device_id_type=MESH
-        )
+    pl.semaphore_wait(barrier, N_MATES - 1)
+    for j in GROUP_MATES:
+        pl.semaphore_signal(ready_sem, inc=1, device_id=ahead(j), device_id_type=MESH)
 
     def send_key(j):
         pltpu.make_async_remote_copy(
@@ -159,12 +149,10 @@
     for j in range(1, N_MATES):
         send_key(j)
 
-    @pl.loop(1, N_SHARD)
-    def _(i):
-        pltpu.make_async_remote_copy(
-            qp_ref, all_qp.at[s], qp_send, qp_recv, (g, lax.rem(s + i, N_SHARD)), MESH
-        ).start()
-
+    for j in SHARD_MATES:
+        pltpu.make_async_remote_copy(
+            qp_ref, all_qp.at[s], qp_send, qp_recv, ahead(j), MESH
+        ).start()
     for j in range(1, N_MATES):
         send_tokens(j)
     for j in range(N_MATES, N_DEV):
@@ -182,29 +170,6 @@
 
     pltpu.make_async_copy(k_all.at[pl.ds(1, BATCH - 1)], k_all.at[pl.ds(1, BATCH - 1)], k_recv.at[0]).wait()
     key_rows(0).start()
-
-    pp_load.wait()
-
-    pltpu.make_async_copy(all_qp.at[pl.ds(0, 15)], all_qp.at[pl.ds(0, 15)], qp_recv).wait()
-    scores = lax.dot_general(
-        all_qp[...].reshape(256, 256), pp_ref[...], (((1,), (1,)), ((), ())),
-        preferred_element_type=jnp.float32,
-    )
-    lane2 = lax.broadcasted_iota(jnp.int32, (256, 128), 1)
-    best = jnp.zeros((256, 128), jnp.float32)
-    for c in range(4):
-        half = scores[:, 128 * (c // 2) : 128 * (c // 2) + 128]
-        top = jnp.max(jnp.where(lane2 // CSIZE == c % 2, half, -jnp.inf), axis=1, keepdims=True)
-        best = jnp.where(lane2 == 4 * s + c, top, best)
-    c_stage[...] = best.reshape(16, 16, 128)
-    c_recv[s] = c_stage[s]
-
-    @pl.loop(1, N_SHARD)
-    def _(i):
-        mate = (s + i) % N_SHARD
-        pltpu.make_async_remote_copy(
-            c_stage.at[mate], c_recv.at[s], c_send, c_rsem, (g, mate), MESH
-        ).start()
 
     pt_load.wait()
 
@@ -259,6 +224,25 @@
     for j in range(1, BATCH):
         back(j)
 
+    pp_load.wait()
+
+    pltpu.make_async_copy(all_qp.at[pl.ds(0, 15)], all_qp.at[pl.ds(0, 15)], qp_recv).wait()
+    scores = lax.dot_general(
+        pp_ref[...], all_qp[...].reshape(256, 256), (((1,), (1,)), ((), ())),
+        preferred_element_type=jnp.float32,
+    )
+    best = jnp.concatenate(
+        [jnp.max(scores[c * CSIZE : (c + 1) * CSIZE], axis=0, keepdims=True) for c in range(4)], axis=0
+    )
+    c_stage[0] = best[:, :128]
+    c_stage[1] = best[:, 128:]
+    c_recv[s] = c_stage[lax.div(s, 8)]
+    for j in SHARD_MATES:
+        to = ahead(j)
+        pltpu.make_async_remote_copy(
+            c_stage.at[lax.div(to[1], 8)], c_recv.at[s], c_send, c_rsem, to, MESH
+        ).start()
+
     @pl.loop(1, N_BATCH - 1)
     def _(b):
         first = b * BATCH
@@ -295,12 +279,20 @@
 
     pltpu.make_async_copy(c_recv.at[pl.ds(0, 15)], c_recv.at[pl.ds(0, 15)], c_rsem).wait()
     probes_load.wait()
-    all_best = jnp.sum(c_recv[...], axis=0)
-    probes = columns(probes_ref)
-    out = jnp.zeros((8, 16), jnp.float32)
+    all_best = c_recv[...]
+    cluster = 4 * lax.broadcasted_iota(jnp.int32, (16, 4, 128), 0) + lax.broadcasted_iota(
+        jnp.int32, (16, 4, 128), 1
+    )
+    first_lane = lax.rem(s, 8) * 16
+    probes = jnp.concatenate([probes_ref[...], jnp.zeros((8, 112), jnp.int32)], axis=1)
+    probes = pltpu.roll(probes, first_lane, 1)
+    row_k = lax.broadcasted_iota(jnp.int32, (8, 128), 0)
+    out = jnp.zeros((8, 128), jnp.float32)
     for k in range(8):
-        pick = jnp.sum(jnp.where(probes[k] == lane, all_best, 0.0), axis=1, keepdims=True)
-        out = jnp.where(row8 == k, across(pick), out)
+        hit = probes[k : k + 1][None] == cluster
+        pick = jnp.sum(jnp.sum(jnp.where(hit, all_best, 0.0), axis=0), axis=0, keepdims=True)
+        out = jnp.where(row_k == k, pick, out)
+    out = pltpu.roll(out, lax.rem(128 - first_lane, 128), 1)[:, :16]
     out_ref[0] = out
 
     pltpu.make_async_copy(r_recv.at[pl.ds(1, 127)], r_recv.at[pl.ds(1, 127)], r_rsem).wait()
@@ -342,8 +334,8 @@
                 pltpu.VMEM((N_DEV, 2, 32, 128), jnp.bfloat16),
                 pltpu.VMEM((N_DEV, 2, 32, 128), jnp.bfloat16),
                 pltpu.VMEM((16, 16, 256), jnp.bfloat16),
-                pltpu.VMEM((16, 16, 128), jnp.float32),
-                pltpu.VMEM((16, 16, 128), jnp.float32),
+                pltpu.VMEM((2, 4, 128), jnp.float32),
+                pltpu.VMEM((16, 4, 128), jnp.float32),
                 pltpu.VMEM((1, 128), jnp.int32),
                 pltpu.VMEM((1, 128), jnp.int32),
                 pltpu.VMEM((N_DEV, 1, 128), jnp.int32),

time: 46.3 us -> 45.6 us (0.985)
  Pallas kernels: 44.2 us -> 43.6 us
    pallas_call x1, Pallas kernels: 44.2 us -> 43.6 us  [body(): pl.pallas_call(kernel, out_shape=jax.ShapeDtypeStruct((2, 8, 16), jnp.flo...]
where the time goes in v5:
time: 45.6 us; the launch traced here: 45.5 us
  Pallas kernels  43.6 us (96%)
  local copies, waits for them, and re-layouts  1.28 us (3%)
  between operations  0.64 us (1%)
    pallas_call x1, Pallas kernels, body(): pl.pallas_call(kernel, out_shape=jax.ShapeDtypeStruct((2, 8, 16), jnp.flo...  43.6 us
    transpose x1, local copies, waits for them, and re-layouts, body(): return (scores[0].T, scores[1].T)  1.28 us

profile of v5, /device:TPU:1, one launch (start us, length us, event | category | flops | bytes accessed | tf_op | source)
XLA Modules:
  0.0 45.5 jit_solution(9531005674965670006)
XLA Ops:
  0.6 43.6 %shard_map.77 = f32[2,8,16]{2,1,0:T(8,128)} custom-call(bf16[16,256]{1,0:T(8,128)(2,1)} %qp_hbm.1, bf16[16,32,128]{2,1,0:T(8,128)(2,1)} %qt_hbm.1, s32[8,16]{1,0:T(8,128)} %bitcast.10, s32[8,16]{1,0:T(8,128)} %bitcast.11, bf16[256,256]{1,0:T(8,128)(2,1)} %pp_hbm.1, bf16[256,128,128]{2,1,0:T(8,128)(2,1)} %pt_hbm.1), custom_call_target="tpu_custom_call" | custom-call | flops 300000000 | bytes 8700000 | tf_op jit(solution)/shard_map/pallas_call | solution.py:322
  44.2 1.3 %slice_bitcast_fusion = (f32[16,8]{0,1:T(8,128)}, f32[16,8]{0,1:T(8,128)}) fusion(f32[2,8,16]{2,1,0:T(8,128)} %shard_map.77), kind=kLoop, calls=%fused_computation | loop fusion | bytes 2048 | tf_op jit(solution)/shard_map/transpose | solution.py:357

commit v6 on v5

--- a/solution.py
+++ b/solution.py
@@ -155,13 +155,12 @@
         ).start()
     for j in range(1, N_MATES):
         send_tokens(j)
-    for j in range(N_MATES, N_DEV):
-        fill(j)
     pl.semaphore_wait(ready_sem, N_GROUP - 1)
     for j in range(N_MATES, N_DEV + LEAD):
         if j < N_DEV:
             send_key(j)
         if j >= N_MATES + LEAD:
+            fill(j - LEAD)
             send_tokens(j - LEAD)
 
     def key_rows(b):

time: 45.6 us -> 45.5 us (level)
  no operation moved by 1% of the time
where the time goes in v6:
time: 45.5 us; the launch traced here: 45.3 us
  Pallas kernels  43.4 us (95%)
  local copies, waits for them, and re-layouts  1.28 us (3%)
  between operations  0.64 us (1%)
    pallas_call x1, Pallas kernels, body(): pl.pallas_call(kernel, out_shape=jax.ShapeDtypeStruct((2, 8, 16), jnp.flo...  43.4 us
    transpose x1, local copies, waits for them, and re-layouts, body(): return (scores[0].T, scores[1].T)  1.28 us

profile of v6, /device:TPU:1, one launch (start us, length us, event | category | flops | bytes accessed | tf_op | source)
XLA Modules:
  0.0 45.3 jit_solution(7002817390323183714)
XLA Ops:
  0.6 43.4 %shard_map.77 = f32[2,8,16]{2,1,0:T(8,128)} custom-call(bf16[16,256]{1,0:T(8,128)(2,1)} %qp_hbm.1, bf16[16,32,128]{2,1,0:T(8,128)(2,1)} %qt_hbm.1, s32[8,16]{1,0:T(8,128)} %bitcast.10, s32[8,16]{1,0:T(8,128)} %bitcast.11, bf16[256,256]{1,0:T(8,128)(2,1)} %pp_hbm.1, bf16[256,128,128]{2,1,0:T(8,128)(2,1)} %pt_hbm.1), custom_call_target="tpu_custom_call" | custom-call | flops 300000000 | bytes 8700000 | tf_op jit(solution)/shard_map/pallas_call | solution.py:321
  44.0 1.3 %slice_bitcast_fusion = (f32[16,8]{0,1:T(8,128)}, f32[16,8]{0,1:T(8,128)}) fusion(f32[2,8,16]{2,1,0:T(8,128)} %shard_map.77), kind=kLoop, calls=%fused_computation | loop fusion | bytes 2048 | tf_op jit(solution)/shard_map/transpose | solution.py:356

commit v7 on v6

--- a/solution.py
+++ b/solution.py
@@ -126,8 +126,6 @@
         stage[j, 0] = qt_ref[v & 15]
         stage[j, 1] = qt_ref[(v >> 4) & 15]
 
-    for j in range(1, N_MATES):
-        fill(j)
 
     qp_load.wait()
     all_qp[s] = qp_ref[...]
@@ -154,6 +152,7 @@
             qp_ref, all_qp.at[s], qp_send, qp_recv, ahead(j), MESH
         ).start()
     for j in range(1, N_MATES):
+        fill(j)
         send_tokens(j)
     pl.semaphore_wait(ready_sem, N_GROUP - 1)
     for j in range(N_MATES, N_DEV + LEAD):

time: 45.5 us -> 45.5 us (level)
  no operation moved by 1% of the time
where the time goes in v7:
time: 45.5 us; the launch traced here: 45.3 us
  Pallas kernels  43.4 us (95%)
  local copies, waits for them, and re-layouts  1.28 us (3%)
  between operations  0.64 us (1%)
    pallas_call x1, Pallas kernels, body(): pl.pallas_call(kernel, out_shape=jax.ShapeDtypeStruct((2, 8, 16), jnp.flo...  43.4 us
    transpose x1, local copies, waits for them, and re-layouts, body(): return (scores[0].T, scores[1].T)  1.28 us

profile of v7, /device:TPU:1, one launch (start us, length us, event | category | flops | bytes accessed | tf_op | source)
XLA Modules:
  0.0 45.3 jit_solution(16106240858415693567)
XLA Ops:
  0.6 43.4 %shard_map.77 = f32[2,8,16]{2,1,0:T(8,128)} custom-call(bf16[16,256]{1,0:T(8,128)(2,1)} %qp_hbm.1, bf16[16,32,128]{2,1,0:T(8,128)(2,1)} %qt_hbm.1, s32[8,16]{1,0:T(8,128)} %bitcast.10, s32[8,16]{1,0:T(8,128)} %bitcast.11, bf16[256,256]{1,0:T(8,128)(2,1)} %pp_hbm.1, bf16[256,128,128]{2,1,0:T(8,128)(2,1)} %pt_hbm.1), custom_call_target="tpu_custom_call" | custom-call | flops 300000000 | bytes 8700000 | tf_op jit(solution)/shard_map/pallas_call | solution.py:320
  44.0 1.3 %slice_bitcast_fusion = (f32[16,8]{0,1:T(8,128)}, f32[16,8]{0,1:T(8,128)}) fusion(f32[2,8,16]{2,1,0:T(8,128)} %shard_map.77), kind=kLoop, calls=%fused_computation | loop fusion | bytes 2048 | tf_op jit(solution)/shard_map/transpose | solution.py:355
